TPU v7x, 32 devices: a whole 2x2x4 slice. The times are simulated.
32 devices in a mesh: segment: 2 (over y), gx: 2 (over x), gy: 8 (over z, core).
Axes of the slice: x: 2, y: 2, z: 4, core: 2. Of those that a mesh axis runs over, the one named last changes fastest.
Arguments:
- node_latent: bfloat16 [16384, 512], P(('segment', 'gx', 'gy')), may hold values from -6 to 6
- edge_latent: bfloat16 [32768, 512], P(('segment', 'gx', 'gy')), may hold values from -6 to 6
- adjacency: bfloat16 [128, 2, 128, 128], P(('segment', 'gx', 'gy')), may hold values from -0.5 to 0.5
- neighbours: int32 [128, 2], P(('segment', 'gx', 'gy')), may hold values from 0 to 9, as said below
- live: int32 [128, 2], P(('segment', 'gx', 'gy')), may hold values 0 or 1
- send_blocks: int32 [32, 6], P(('segment', 'gx', 'gy')), may hold values from 0 to 3
- w_edge_in: bfloat16 [1536, 512], replicated, may hold values from -0.15625 to 0.15625
- w_edge_out: bfloat16 [512, 512], replicated, may hold values from -0.25 to 0.25
- w_node_in: bfloat16 [1024, 512], replicated, may hold values from -0.1875 to 0.1875
- w_node_out: bfloat16 [512, 512], replicated, may hold values from -0.25 to 0.25
- node_cotangent: bfloat16 [16384, 512], P(('segment', 'gx', 'gy')), may hold values from -6 to 6
- edge_cotangent: bfloat16 [32768, 512], P(('segment', 'gx', 'gy')), may hold values from -6 to 6
Outputs:
- node_out: bfloat16 [16384, 512], P(('segment', 'gx', 'gy'))
- edge_out: bfloat16 [32768, 512], P(('segment', 'gx', 'gy'))
- node_grad: float32 [16384, 512], P(('segment', 'gx', 'gy'))
- grad_edge_in: float32 [786432], P(('segment', 'gx', 'gy'))
- grad_edge_out: float32 [262144], P(('segment', 'gx', 'gy'))
- grad_node_in: float32 [524288], P(('segment', 'gx', 'gy'))
- grad_node_out: float32 [262144], P(('segment', 'gx', 'gy'))
Inputs may be any that keep to these rules, and one draw needn't show every extreme that they name: `neighbours`: indices below 4 name the device's own blocks, 4 + j names received block j; on every device each of the six received blocks is named by at least one slot.
All inputs are finite; a program needn't handle non-finite values. No bound on the sum of `live` on one device may be relied on, other than what follows from the above.
Results may differ from a plain program's by a relative error of at most 0.014.
Values may be sent and summed in bfloat16 or wider, within the bound.
A program may use at most 128 MiB of HBM per device.

v0:
```python
from functools import partial

import jax
import jax.numpy as jnp
from jax import lax
from jax.sharding import PartitionSpec as P


def passed_along(block, axis, distance):
    devices = range(lax.axis_size(axis))
    route = [(i - distance, i) for i in devices if i - distance in devices]
    return lax.ppermute(block, axis, route)


def layer_norm(values):
    average = jnp.mean(values, axis=-1, keepdims=True)
    centred = values - average
    return centred * lax.rsqrt(jnp.mean(centred * centred, axis=-1, keepdims=True) + 1e-05)


def edge_part(node_blocks, received, w_edge_in, w_edge_out, edge_rows, adjacency_tiles, picker):
    latent = node_blocks.shape[-1]
    blocks = node_blocks.shape[0]
    block_rows = node_blocks.shape[1]
    degree = picker.shape[0] // blocks
    extended = jnp.concatenate([node_blocks, received], axis=0)
    sources = jnp.einsum(
        "sn,nbd->sbd", picker, extended, preferred_element_type=jnp.float32
    ).astype(jnp.bfloat16)
    mixed_rows = jnp.einsum(
        "sij,sjd->sid", adjacency_tiles, sources, preferred_element_type=jnp.float32
    ).astype(jnp.bfloat16)
    self_term = jnp.dot(
        node_blocks.reshape(-1, latent),
        w_edge_in[latent : 2 * latent],
        preferred_element_type=jnp.float32,
    )
    pre_edge = jnp.dot(edge_rows, w_edge_in[:latent], preferred_element_type=jnp.float32) + jnp.dot(
        mixed_rows.reshape(-1, latent), w_edge_in[2 * latent :], preferred_element_type=jnp.float32
    )
    pre_edge = (
        pre_edge.reshape(blocks, degree, block_rows, latent)
        + self_term.reshape(blocks, 1, block_rows, latent)
    ).reshape(-1, latent)
    edge_hidden = jax.nn.silu(pre_edge).astype(jnp.bfloat16)
    return layer_norm(jnp.dot(edge_hidden, w_edge_out, preferred_element_type=jnp.float32))


def node_part(node_blocks, messages, w_node_in, w_node_out, edge_rows, live_weight):
    latent = node_blocks.shape[-1]
    blocks = node_blocks.shape[0]
    block_rows = node_blocks.shape[1]
    edges_out = (edge_rows.astype(jnp.float32) + messages).astype(jnp.bfloat16)
    gathered = jnp.sum(
        messages.reshape(blocks, -1, block_rows, latent) * live_weight[:, :, None, None], axis=1
    ).astype(jnp.bfloat16)
    flat_nodes = node_blocks.reshape(-1, latent)
    pre_node = jnp.dot(
        flat_nodes, w_node_in[:latent], preferred_element_type=jnp.float32
    ) + jnp.dot(
        gathered.reshape(-1, latent), w_node_in[latent:], preferred_element_type=jnp.float32
    )
    node_hidden = jax.nn.silu(pre_node).astype(jnp.bfloat16)
    nodes_out = (
        flat_nodes.astype(jnp.float32)
        + layer_norm(jnp.dot(node_hidden, w_node_out, preferred_element_type=jnp.float32))
    ).astype(jnp.bfloat16)
    return (nodes_out, edges_out)


def across_rows(face_rows, offset):
    return passed_along(face_rows, "gx", offset)


def across_cols(face_rows, offset):
    return passed_along(face_rows, "gy", offset)


def across_segment(face_rows, offset):
    return passed_along(face_rows, "segment", offset)


def swap_faces(face_blocks):
    return jnp.stack(
        [
            across_rows(face_blocks[1], 1),
            across_rows(face_blocks[0], -1),
            across_cols(face_blocks[3], 1),
            across_cols(face_blocks[2], -1),
            across_segment(face_blocks[5], 1),
            across_segment(face_blocks[4], -1),
        ],
        axis=0,
    )


def shards(
    node_latent,
    edge_latent,
    adjacency,
    neighbours,
    live,
    send_blocks,
    w_edge_in,
    w_edge_out,
    w_node_in,
    w_node_out,
    node_cotangent,
    edge_cotangent,
):
    latent = node_latent.shape[1]
    blocks, degree = neighbours.shape
    block_rows = adjacency.shape[-1]
    node_blocks = node_latent.reshape(blocks, block_rows, latent)
    choose = (send_blocks[0][:, None] == jnp.arange(blocks, dtype=jnp.int32)[None, :]).astype(
        jnp.bfloat16
    )
    outgoing = jnp.einsum(
        "jn,nbd->jbd", choose, node_blocks, preferred_element_type=jnp.float32
    ).astype(jnp.bfloat16)
    received = swap_faces(outgoing)
    adjacency_tiles = adjacency.reshape(blocks * degree, block_rows, block_rows)
    picker = (
        neighbours.reshape(-1)[:, None] == jnp.arange(blocks + 6, dtype=jnp.int32)[None, :]
    ).astype(jnp.bfloat16)
    live_weight = live.astype(jnp.float32)
    messages, edge_pull = jax.vjp(
        partial(edge_part, edge_rows=edge_latent, adjacency_tiles=adjacency_tiles, picker=picker),
        node_blocks,
        received,
        w_edge_in,
        w_edge_out,
    )
    outputs, node_pull = jax.vjp(
        partial(node_part, edge_rows=edge_latent, live_weight=live_weight),
        node_blocks,
        messages,
        w_node_in,
        w_node_out,
    )
    node_direct, message_ct, grad_ni, grad_no = node_pull((node_cotangent, edge_cotangent))
    node_terms = (grad_ni.astype(jnp.float32).reshape(-1), grad_no.astype(jnp.float32).reshape(-1))
    node_indirect, received_ct, grad_ei, grad_eo = edge_pull(message_ct)
    returned = swap_faces(received_ct)
    node_grad = node_direct.astype(jnp.float32) + node_indirect.astype(jnp.float32)
    node_grad = node_grad + jnp.einsum(
        "jn,jbd->nbd", choose, returned, preferred_element_type=jnp.float32
    )
    edge_terms = (grad_ei.astype(jnp.float32).reshape(-1), grad_eo.astype(jnp.float32).reshape(-1))
    shares = (
        lax.psum_scatter(edge_terms[0], ("segment", "gx", "gy"), scatter_dimension=0, tiled=True),
        lax.psum_scatter(edge_terms[1], ("segment", "gx", "gy"), scatter_dimension=0, tiled=True),
        lax.psum_scatter(node_terms[0], ("segment", "gx", "gy"), scatter_dimension=0, tiled=True),
        lax.psum_scatter(node_terms[1], ("segment", "gx", "gy"), scatter_dimension=0, tiled=True),
    )
    return (
        outputs[0],
        outputs[1],
        node_grad.reshape(-1, latent),
        shares[0],
        shares[1],
        shares[2],
        shares[3],
    )


def solution(mesh):
    placed = (
        P(("segment", "gx", "gy"), None),
        P(("segment", "gx", "gy"), None),
        P(("segment", "gx", "gy"), None, None, None),
        P(("segment", "gx", "gy"), None),
        P(("segment", "gx", "gy"), None),
        P(("segment", "gx", "gy"), None),
        P(),
        P(),
        P(),
        P(),
        P(("segment", "gx", "gy"), None),
        P(("segment", "gx", "gy"), None),
    )
    return jax.shard_map(
        shards,
        mesh=mesh,
        in_specs=placed,
        out_specs=(
            P(("segment", "gx", "gy"), None),
            P(("segment", "gx", "gy"), None),
            P(("segment", "gx", "gy"), None),
            P(("segment", "gx", "gy")),
            P(("segment", "gx", "gy")),
            P(("segment", "gx", "gy")),
            P(("segment", "gx", "gy")),
        ),
        check_vma=False,
    )
```

profile of v0, /device:TPU:0, one launch (start us, length us, event | category | flops | bytes accessed | tf_op | source)
XLA Modules:
  0.0 282.6 jit_solution(11788495208928686759)
XLA Ops:
  7.2 1.7 convolution_convert_fusion.4
  10.1 4.8 %collective-permute-start = (bf16[128,512]{1,0:T(8,128)(2,1)S(1)}, bf16[128,512]{1,0:T(8,128)(2,1)S(1)}, u32[]{:S(2)}, u32[]{:S(2)}) collective-permute-start(bf16[128,512]{1,0:T(8,128)(2,1)S(1)} %bitcast.163), channel_id=1, source_target_pairs={{0,8},{1,9},{2,10},{3,11},{4,12},{5,13},{6,14},{7,15},{16,24},{17,... | collective-permute-start | bytes 393224 | tf_op jit(solution)/shard_map/ppermute | solution.py:12
  15.0 1.3 collective-permute-start.1
  17.0 2.1 collective-permute-start.2
  19.8 1.4 collective-permute-start.3
  21.8 4.1 %collective-permute-start.4 = (bf16[128,512]{1,0:T(8,128)(2,1)}, bf16[128,512]{1,0:T(8,128)(2,1)}, u32[]{:S(2)}, u32[]{:S(2)}) collective-permute-start(bf16[128,512]{1,0:T(8,128)(2,1)} %bitcast.131), channel_id=1, source_target_pairs={{0,16},{1,17},{2,18},{3,19},{4,20},{5,21},{6,22},{7,23},{8,24},{9,... | collective-permute-start | bytes 393224 | tf_op jit(solution)/shard_map/ppermute | solution.py:12
  25.9 2.0 fusion.38
  28.0 1.4 fusion.43
  30.0 1.5 collective-permute-start.5
  31.5 1.4 fusion.48
  37.7 1.8 copy.207
  39.5 1.8 copy.208
  41.3 1.8 copy.209
  43.1 1.8 copy.210
  44.9 10.9 %concatenate.3 = bf16[10,128,512]{2,0,1:T(8,128)(2,1)} concatenate(bf16[4,128,512]{2,0,1:T(4,128)(2,1)} %copy.204, bf16[1,128,512]{2,0,1:T(2,128)(2,1)} %copy.205, bf16[1,128,512]{2,0,1:T(2,128)(2,1)} %copy.206, bf16[1,128,512]{2,0,1:T(2,128)(2,1)} %copy.207, bf16[1,128,512]{2,0,1:T(2,128)(2,1)} %copy.208, bf16[1,128,512]{2,0,1:T(2,128)(2,1)} %copy.209, bf16[1,128,512]{2,0,1:T(2,128)(2,1)} %copy.210), dimensions={0} | concatenate | bytes 2621440 | tf_op jit(solution)/shard_map/jvp()/concatenate | solution.py:26
  55.8 2.2 convolution_convert_fusion.5
  58.9 1.8 bitcast_add_fusion
  62.0 1.4 add_convert_fusion
  70.5 1.5 fusion.66
  72.1 1.3 fusion
  73.4 1.6 fusion.25
  75.0 1.6 fusion.71
  76.6 2.0 fusion.17
  78.5 1.3 fusion.24
  81.1 1.8 fusion.21
  84.0 1.5 fusion.23
  85.6 1.5 convert_bitcast_fusion
  87.1 2.5 copy.246
  91.1 1.9 copy.248
  94.3 1.8 convolution_convert_fusion.1
  96.6 1.7 copy.216
  98.3 2.0 convolution_convert_fusion
  101.6 4.5 %collective-permute-start.6 = (bf16[128,512]{1,0:T(8,128)(2,1)S(1)}, bf16[128,512]{1,0:T(8,128)(2,1)S(1)}, u32[]{:S(2)}, u32[]{:S(2)}) collective-permute-start(bf16[128,512]{1,0:T(8,128)(2,1)S(1)} %bitcast.164), channel_id=1, source_target_pairs={{0,8},{1,9},{2,10},{3,11},{4,12},{5,13},{6,14},{7,15},{16,24},{17,... | collective-permute-start | bytes 393224 | tf_op jit(solution)/shard_map/ppermute | solution.py:12
  106.7 1.4 collective-permute-start.7
  108.8 4.3 %collective-permute-start.8 = (bf16[128,512]{1,0:T(8,128)(2,1)}, bf16[128,512]{1,0:T(8,128)(2,1)}, u32[]{:S(2)}, u32[]{:S(2)}) collective-permute-start(bf16[128,512]{1,0:T(8,128)(2,1)} %bitcast.127), channel_id=1, source_target_pairs={{0,1},{1,2},{2,3},{3,4},{4,5},{5,6},{6,7},{8,9},{9,10},{10,11},{11... | collective-permute-start | bytes 393224 | tf_op jit(solution)/shard_map/ppermute | solution.py:12
  113.8 1.3 collective-permute-start.9
  115.7 5.4 %collective-permute-start.10 = (bf16[128,512]{1,0:T(8,128)(2,1)}, bf16[128,512]{1,0:T(8,128)(2,1)}, u32[]{:S(2)}, u32[]{:S(2)}) collective-permute-start(bf16[128,512]{1,0:T(8,128)(2,1)} %bitcast.125), channel_id=1, source_target_pairs={{0,16},{1,17},{2,18},{3,19},{4,20},{5,21},{6,22},{7,23},{8,24},{9,... | collective-permute-start | bytes 393224 | tf_op jit(solution)/shard_map/ppermute | solution.py:12
  121.7 1.3 collective-permute-start.11
  123.0 2.3 convolution_convert_fusion.12
  131.3 1.8 copy.224
  133.2 5.6 %stack.51 = bf16[6,128,512]{2,0,1:T(8,128)(2,1)} concatenate(bf16[1,128,512]{2,0,1:T(2,128)(2,1)S(1)} %copy.219, bf16[1,128,512]{2,0,1:T(2,128)(2,1)S(1)} %copy.220, bf16[1,128,512]{2,0,1:T(2,128)(2,1)S(1)} %copy.221, bf16[1,128,512]{2,0,1:T(2,128)(2,1)S(1)} %copy.222, bf16[1,128,512]{2,0,1:T(2,128)(2,1)S(1)} %copy.223, bf16[1,128,512]{2,0,1:T(2,128)(2,1)} %copy.224), dimensions={0} | concatenate | bytes 1572864 | tf_op jit(solution)/shard_map/stack | solution.py:84
  138.8 2.9 %convolution_add_fusion = f32[4,128,512]{2,0,1:T(4,128)S(1)} fusion(bf16[6,128,512]{2,0,1:T(8,128)(2,1)} %stack.51, f32[4,128,512]{2,1,0:T(8,128)} %convert.6, bf16[10,128,512]{2,0,1:T(8,128)(2,1)S(1)} %convolution_convert_fusion, bf16[4,128,512]{2,1,0:T(8,128)(2,1)} %bitcast.155, s32[6]{0:T(128)S(1)} %bitcast.168), kind=kOutput, calls=%fused_computation.32 | convolution fusion | flops 4194328 | bytes 3932184 | tf_op jit(solution)/shard_map/jn,jbd->nbd/dot_general | solution.py:146
  141.7 1.3 copy.225
  143.0 127.0 %all-reduce.12.cloned.1.call-done = (f32[786432]{0:T(1024)}, f32[262144]{0:T(1024)}, f32[524288]{0:T(1024)}, f32[262144]{0:T(1024)}) async-done(((f32[786432]{0:T(1024)}, f32[262144]{0:T(1024)}, f32[524288]{0:T(1024)}, f32[262144]{0:T(1024)}), (f32[786432]{0:T(1024)}, f32[262144]{0:T(1024)}, f32[524288]{0:T(1024)}, f32[262144]{0:T(1024)})) %all-reduce.12.cloned.1.call-update) | async-done | bytes 7340048
  270.0 1.4 dynamic-slice.1
  271.3 1.4 dynamic-slice.3
  272.7 1.5 dynamic-slice
  274.3 1.5 dynamic-slice.2
  (130 shorter events, 33.9 us)
Async XLA Ops:
  7.2 53.5 %copy-start = (bf16[512,512]{1,0:T(8,128)(2,1)S(1)}, bf16[512,512]{1,0:T(8,128)(2,1)}, u32[]{:S(2)}) copy-start(bf16[512,512]{1,0:T(8,128)(2,1)} %param.19) | copy-start | bytes 1572868
  7.2 262.8 %all-reduce.12.cloned.1.call-start = ((), (), s32[]{:S(2)}) async-start(), calls=%async_computation | async-start | bytes 14680064
  8.9 17.0 %copy-start.3 = (bf16[1024,512]{1,0:T(8,128)(2,1)S(1)}, bf16[1024,512]{1,0:T(8,128)(2,1)}, u32[]{:S(2)}) copy-start(bf16[1024,512]{1,0:T(8,128)(2,1)} %param.13) | copy-start | bytes 3145732
  8.9 17.0 %copy-start.11 = (bf16[1536,512]{1,0:T(8,128)(2,1)S(1)}, bf16[1536,512]{1,0:T(8,128)(2,1)}, u32[]{:S(2)}) copy-start(bf16[1536,512]{1,0:T(8,128)(2,1)} %param.18) | copy-start | bytes 4718596
  10.1 19.9 %collective-permute-start = (bf16[128,512]{1,0:T(8,128)(2,1)S(1)}, bf16[128,512]{1,0:T(8,128)(2,1)S(1)}, u32[]{:S(2)}, u32[]{:S(2)}) collective-permute-start(bf16[128,512]{1,0:T(8,128)(2,1)S(1)} %bitcast.163), channel_id=1, source_target_pairs={{0,8},{1,9},{2,10},{3,11},{4,12},{5,13},{6,14},{7,15},{16,24},{17,... | collective-permute-start | bytes 393224 | tf_op jit(solution)/shard_map/ppermute | solution.py:12
  15.0 21.8 %collective-permute-start.1 = (bf16[128,512]{1,0:T(8,128)(2,1)S(1)}, bf16[128,512]{1,0:T(8,128)(2,1)S(1)}, u32[]{:S(2)}, u32[]{:S(2)}) collective-permute-start(bf16[128,512]{1,0:T(8,128)(2,1)S(1)} %bitcast.158), channel_id=1, source_target_pairs={{8,0},{9,1},{10,2},{11,3},{12,4},{13,5},{14,6},{15,7},{24,16},{25,... | collective-permute-start | bytes 393224 | tf_op jit(solution)/shard_map/ppermute | solution.py:12
  17.0 20.7 %collective-permute-start.2 = (bf16[128,512]{1,0:T(8,128)(2,1)}, bf16[128,512]{1,0:T(8,128)(2,1)}, u32[]{:S(2)}, u32[]{:S(2)}) collective-permute-start(bf16[128,512]{1,0:T(8,128)(2,1)} %bitcast.133), channel_id=1, source_target_pairs={{0,1},{1,2},{2,3},{3,4},{4,5},{5,6},{6,7},{8,9},{9,10},{10,11},{11... | collective-permute-start | bytes 393224 | tf_op jit(solution)/shard_map/ppermute | solution.py:12
  19.8 8.2 %copy-start.2 = (bf16[512,512]{1,0:T(8,128)(2,1)S(1)}, bf16[512,512]{1,0:T(8,128)(2,1)}, u32[]{:S(2)}) copy-start(bf16[512,512]{1,0:T(8,128)(2,1)} %param.12) | copy-start | bytes 1572868
  19.8 19.8 %collective-permute-start.3 = (bf16[128,512]{1,0:T(8,128)(2,1)}, bf16[128,512]{1,0:T(8,128)(2,1)}, u32[]{:S(2)}, u32[]{:S(2)}) collective-permute-start(bf16[128,512]{1,0:T(8,128)(2,1)} %bitcast.132), channel_id=1, source_target_pairs={{1,0},{2,1},{3,2},{4,3},{5,4},{6,5},{7,6},{9,8},{10,9},{11,10},{12... | collective-permute-start | bytes 393224 | tf_op jit(solution)/shard_map/ppermute | solution.py:12
  21.8 19.5 %collective-permute-start.4 = (bf16[128,512]{1,0:T(8,128)(2,1)}, bf16[128,512]{1,0:T(8,128)(2,1)}, u32[]{:S(2)}, u32[]{:S(2)}) collective-permute-start(bf16[128,512]{1,0:T(8,128)(2,1)} %bitcast.131), channel_id=1, source_target_pairs={{0,16},{1,17},{2,18},{3,19},{4,20},{5,21},{6,22},{7,23},{8,24},{9,... | collective-permute-start | bytes 393224 | tf_op jit(solution)/shard_map/ppermute | solution.py:12
  28.0 3.6 %copy-start.12 = (bf16[1024,512]{1,0:T(8,128)(2,1)S(1)}, bf16[1024,512]{1,0:T(8,128)(2,1)}, u32[]{:S(2)}) copy-start(bf16[1024,512]{1,0:T(8,128)(2,1)} %param.20) | copy-start | bytes 3145732
  30.0 13.1 %collective-permute-start.5 = (bf16[128,512]{1,0:T(8,128)(2,1)}, bf16[128,512]{1,0:T(8,128)(2,1)}, u32[]{:S(2)}, u32[]{:S(2)}) collective-permute-start(bf16[128,512]{1,0:T(8,128)(2,1)} %bitcast.130), channel_id=1, source_target_pairs={{16,0},{17,1},{18,2},{19,3},{20,4},{21,5},{22,6},{23,7},{24,8},{25... | collective-permute-start | bytes 393224 | tf_op jit(solution)/shard_map/ppermute | solution.py:12
  32.9 2.7 copy-start.27
  32.9 2.9 %copy-start.28 = (s32[4,2]{0,1:T(2,128)S(1)}, s32[4,2]{0,1:T(2,128)}, u32[]{:S(2)}) copy-start(s32[4,2]{0,1:T(2,128)} %param.16) | copy-start | bytes 100
  35.6 31.9 %copy-start.6 = (bf16[512,512]{0,1:T(8,128)(2,1)}, bf16[512,512]{0,1:T(8,128)(2,1)S(1)}, u32[]{:S(2)}) copy-start(bf16[512,512]{0,1:T(8,128)(2,1)S(1)} %copy.213) | copy-start | bytes 1572868
  44.9 13.1 %copy-start.21 = (bf16[4,2,128,128]{3,2,1,0:T(8,128)(2,1)S(1)}, bf16[4,2,128,128]{3,2,1,0:T(8,128)(2,1)}, u32[]{:S(2)}) copy-start(bf16[4,2,128,128]{3,2,1,0:T(8,128)(2,1)} %param.14) | copy-start | bytes 786436
  55.8 3.1 %copy-start.5 = (f32[1024,512]{1,0:T(8,128)S(1)}, f32[1024,512]{1,0:T(8,128)}, u32[]{:S(2)}) copy-start(f32[1024,512]{1,0:T(8,128)} %fusion.38) | copy-start | bytes 6291460
  55.8 3.1 %copy-start.10 = (f32[512,512]{1,0:T(8,128)S(1)}, f32[512,512]{1,0:T(8,128)}, u32[]{:S(2)}) copy-start(f32[512,512]{1,0:T(8,128)} %fusion.43) | copy-start | bytes 3145732
  63.4 1.2 copy-start.8
  63.4 1.5 copy-start.13
  63.8 1.6 copy-start.29
  68.2 11.6 %copy-start.17 = (bf16[512,512]{1,0:T(8,128)(2,1)}, bf16[512,512]{1,0:T(8,128)(2,1)S(1)}, u32[]{:S(2)}) copy-start(bf16[512,512]{1,0:T(8,128)(2,1)S(1)} %fusion.29) | copy-start | bytes 1572868
  68.2 1.4 copy-start.9
  72.1 1.3 copy-start.4
  78.5 2.5 copy-start.7
  82.9 2.7 copy-start.15
  87.0 2.5 copy-start.22
  89.5 1.3 copy-start.20
  89.5 1.3 copy-start.25
  91.1 1.9 copy-start.23
  100.3 5.8 %copy-start.14 = (bf16[1024,512]{1,0:T(8,128)(2,1)S(1)}, bf16[1024,512]{1,0:T(8,128)(2,1)}, u32[]{:S(2)}) copy-start(bf16[1024,512]{1,0:T(8,128)(2,1)} %param.20) | copy-start | bytes 3145732
  100.3 5.8 %copy-start.18 = (bf16[512,512]{1,0:T(8,128)(2,1)S(1)}, bf16[512,512]{1,0:T(8,128)(2,1)}, u32[]{:S(2)}) copy-start(bf16[512,512]{1,0:T(8,128)(2,1)} %copy-done.17) | copy-start | bytes 1572868
  100.4 5.8 %copy-start.24 = (bf16[512,512]{1,0:T(8,128)(2,1)S(1)}, bf16[512,512]{1,0:T(8,128)(2,1)}, u32[]{:S(2)}) copy-start(bf16[512,512]{1,0:T(8,128)(2,1)} %param.22) | copy-start | bytes 1572868
  101.6 21.4 %copy-start.19 = (bf16[4,128,512]{2,1,0:T(8,128)(2,1)S(1)}, bf16[4,128,512]{2,1,0:T(8,128)(2,1)}, u32[]{:S(2)}) copy-start(bf16[4,128,512]{2,1,0:T(8,128)(2,1)} %reduce_sum.115) | copy-start | bytes 1572868
  101.6 20.1 %collective-permute-start.6 = (bf16[128,512]{1,0:T(8,128)(2,1)S(1)}, bf16[128,512]{1,0:T(8,128)(2,1)S(1)}, u32[]{:S(2)}, u32[]{:S(2)}) collective-permute-start(bf16[128,512]{1,0:T(8,128)(2,1)S(1)} %bitcast.164), channel_id=1, source_target_pairs={{0,8},{1,9},{2,10},{3,11},{4,12},{5,13},{6,14},{7,15},{16,24},{17,... | collective-permute-start | bytes 393224 | tf_op jit(solution)/shard_map/ppermute | solution.py:12
  106.7 18.7 %copy-start.16 = (bf16[512,512]{0,1:T(8,128)(2,1)S(1)}, bf16[512,512]{0,1:T(8,128)(2,1)}, u32[]{:S(2)}) copy-start(bf16[512,512]{0,1:T(8,128)(2,1)} %get-tuple-element.87) | copy-start | bytes 1572868
  106.7 21.0 %collective-permute-start.7 = (bf16[128,512]{1,0:T(8,128)(2,1)S(1)}, bf16[128,512]{1,0:T(8,128)(2,1)S(1)}, u32[]{:S(2)}, u32[]{:S(2)}) collective-permute-start(bf16[128,512]{1,0:T(8,128)(2,1)S(1)} %bitcast.161), channel_id=1, source_target_pairs={{8,0},{9,1},{10,2},{11,3},{12,4},{13,5},{14,6},{15,7},{24,16},{25,... | collective-permute-start | bytes 393224 | tf_op jit(solution)/shard_map/ppermute | solution.py:12
  108.8 19.1 %collective-permute-start.8 = (bf16[128,512]{1,0:T(8,128)(2,1)}, bf16[128,512]{1,0:T(8,128)(2,1)}, u32[]{:S(2)}, u32[]{:S(2)}) collective-permute-start(bf16[128,512]{1,0:T(8,128)(2,1)} %bitcast.127), channel_id=1, source_target_pairs={{0,1},{1,2},{2,3},{3,4},{4,5},{5,6},{6,7},{8,9},{9,10},{10,11},{11... | collective-permute-start | bytes 393224 | tf_op jit(solution)/shard_map/ppermute | solution.py:12
  113.8 15.3 %collective-permute-start.9 = (bf16[128,512]{1,0:T(8,128)(2,1)}, bf16[128,512]{1,0:T(8,128)(2,1)}, u32[]{:S(2)}, u32[]{:S(2)}) collective-permute-start(bf16[128,512]{1,0:T(8,128)(2,1)} %bitcast.126), channel_id=1, source_target_pairs={{1,0},{2,1},{3,2},{4,3},{5,4},{6,5},{7,6},{9,8},{10,9},{11,10},{12... | collective-permute-start | bytes 393224 | tf_op jit(solution)/shard_map/ppermute | solution.py:12
  115.7 14.5 %collective-permute-start.10 = (bf16[128,512]{1,0:T(8,128)(2,1)}, bf16[128,512]{1,0:T(8,128)(2,1)}, u32[]{:S(2)}, u32[]{:S(2)}) collective-permute-start(bf16[128,512]{1,0:T(8,128)(2,1)} %bitcast.125), channel_id=1, source_target_pairs={{0,16},{1,17},{2,18},{3,19},{4,20},{5,21},{6,22},{7,23},{8,24},{9,... | collective-permute-start | bytes 393224 | tf_op jit(solution)/shard_map/ppermute | solution.py:12
  121.7 9.6 %collective-permute-start.11 = (bf16[128,512]{1,0:T(8,128)(2,1)}, bf16[128,512]{1,0:T(8,128)(2,1)}, u32[]{:S(2)}, u32[]{:S(2)}) collective-permute-start(bf16[128,512]{1,0:T(8,128)(2,1)} %bitcast.124), channel_id=1, source_target_pairs={{16,0},{17,1},{18,2},{19,3},{20,4},{21,5},{22,6},{23,7},{24,8},{25... | collective-permute-start | bytes 393224 | tf_op jit(solution)/shard_map/ppermute | solution.py:12
  128.0 10.8 %copy-start.26 = (s32[1,6]{1,0:T(1,128)S(1)}, s32[1,6]{1,0:T(1,128)}, u32[]{:S(2)}) copy-start(s32[1,6]{1,0:T(1,128)} %param.17) | copy-start | bytes 76
  138.8 137.0 %copy-start.1 = (bf16[512,512]{1,0:T(8,128)(2,1)S(1)}, bf16[512,512]{1,0:T(8,128)(2,1)}, u32[]{:S(2)}) copy-start(bf16[512,512]{1,0:T(8,128)(2,1)} %param.19) | copy-start | bytes 1572868
Sparse Core Ops, SparseCore 0:
  94.4 175.4 all-reduce.11
where the time goes:
time: 285 us; the launch traced here: 283 us
  waiting for transfers between devices  127 us (45%)
  local copies, waits for them, and re-layouts  60.7 us (21%)
  matrix products  36.8 us (13%)
  starting transfers between devices  33.4 us (12%)
  between operations  14.7 us (5%)
  other arithmetic  10.1 us (4%)
    unnamed x2, waiting for transfers between devices  127 us
    ppermute x12, starting transfers between devices, passed_along(): return lax.ppermute(block, axis, route)  33.3 us
    unnamed x84, local copies, waits for them, and re-layouts  22.8 us
    another operation x13, local copies, waits for them, and re-layouts, swap_faces(): jnp.stack([across_rows(face_blocks[1], 1), across_rows(face_blocks[0], -1...  20.2 us
    concatenate x1, local copies, waits for them, and re-layouts, edge_part(): extended = jnp.concatenate([node_blocks, received], axis=0)  10.9 us
  transfers between devices with their start and end apart: 13, of which 1 were waited for; matrix products, arithmetic and copies ran while one was open for 17% of the time, Pallas kernels for 0%

commit v1 on v0

v1 whole, which is shorter than its diff:
```python
import functools

import jax
import jax.numpy as jnp
from jax import lax
from jax.experimental import pallas as pl
from jax.experimental.pallas import tpu as pltpu
from jax.sharding import PartitionSpec as P

AXES = ("segment", "gx", "gy")
FACES = ("gx", "gy", "segment")
MESH = pl.DeviceIdType.MESH
F32 = jnp.float32
BF16 = jnp.bfloat16
CORES = 2
TILE = 16


def mm(a, b):
    return lax.dot_general(a, b, (((1,), (0,)), ((), ())), preferred_element_type=F32)


def mm_nt(a, b):
    return lax.dot_general(a, b, (((1,), (1,)), ((), ())), preferred_element_type=F32)


def mm_tn(a, b):
    return lax.dot_general(a, b, (((0,), (0,)), ((), ())), preferred_element_type=F32)


def normalised(values):
    centred = values - jnp.mean(values, axis=-1, keepdims=True)
    scale = lax.rsqrt(jnp.mean(centred * centred, axis=-1, keepdims=True) + 1e-05)
    return centred * scale, scale


def normalised_ct(ct, unit, scale):
    return scale * (
        ct
        - jnp.mean(ct, axis=-1, keepdims=True)
        - unit * jnp.mean(ct * unit, axis=-1, keepdims=True)
    )


def silu_and_slope(v):
    gate = 0.5 * jnp.tanh(0.5 * v) + 0.5
    value = v * gate
    return value, gate + value * (1.0 - gate)


class Halo:
    def __init__(self, source, target, sems, first, sizes):
        self.links = []
        for a, axis in enumerate(FACES):
            here = lax.axis_index(axis)
            for step, out, into in ((1, 2 * a + 1, 2 * a), (-1, 2 * a, 2 * a + 1)):
                other = here + step
                to = (other >= 0) & (other < sizes[axis])
                back = here - step
                frm = (back >= 0) & (back < sizes[axis])
                copy = pltpu.make_async_remote_copy(
                    src_ref=source.at[out],
                    dst_ref=target.at[into],
                    send_sem=sems.at[0, first + into],
                    recv_sem=sems.at[1, first + into],
                    device_id={axis: other},
                    device_id_type=MESH,
                )
                self.links.append((to, frm, copy, into))
        self.target = target

    def start(self):
        for to, frm, copy, into in self.links:
            pl.when(to)(copy.start)

    def zero(self):
        for to, frm, copy, into in self.links:

            @pl.when(jnp.logical_not(frm))
            def _(into=into):
                self.target[into] = jnp.zeros(self.target.shape[1:], self.target.dtype)

    def arrive(self):
        for to, frm, copy, into in self.links:
            pl.when(frm)(copy.wait_recv)

    def sent(self):
        for to, frm, copy, into in self.links:
            pl.when(to)(copy.wait_send)


class Scatter:
    def __init__(self, full, r1, r2, r3, rz, sems, piece, sizes):
        self.full, self.r1, self.r2, self.r3, self.rz = full, r1, r2, r3, rz
        self.depth = sizes["gy"] // CORES
        self.seg, self.gx = lax.axis_index("segment"), lax.axis_index("gx")
        gy = lax.axis_index("gy")
        self.core, self.z = lax.rem(gy, CORES), lax.div(gy, CORES)
        self.sem = lambda side, k: sems.at[side, piece, k]

    def copy(self, src, dst, k, to):
        return pltpu.make_async_remote_copy(
            src_ref=src,
            dst_ref=dst,
            send_sem=self.sem(0, k),
            recv_sem=self.sem(1, k),
            device_id=to,
            device_id_type=MESH,
        )

    def core_copy(self):
        other = 1 - self.core
        return self.copy(
            self.full.at[:, :, :, other], self.r1, 0, {"gy": self.z * CORES + other}
        )

    def first_copy(self, core):
        if core == 0:
            return self.copy(self.r1.at[:, 1 - self.gx], self.r2, 1, {"gx": 1 - self.gx})
        return self.copy(self.r1.at[1 - self.seg], self.r2, 1, {"segment": 1 - self.seg})

    def second_copy(self, core):
        if core == 0:
            return self.copy(self.r2.at[1 - self.seg], self.r3, 2, {"segment": 1 - self.seg})
        return self.copy(self.r2.at[1 - self.gx], self.r3, 2, {"gx": 1 - self.gx})

    def last_copy(self, step):
        to = lax.rem(self.z + step, self.depth)
        return self.copy(
            self.r3.at[to], self.rz.at[step - 1], 2 + step, {"gy": to * CORES + self.core}
        )

    def by_core(self, act):
        for core in range(CORES):
            pl.when(self.core == core)(functools.partial(act, core))

    def start(self):
        self.core_copy().start()

    def step1(self):
        self.core_copy().wait_recv()
        for s in range(2):
            for x in range(2):

                def body(z, _):
                    self.r1[s, x, z] = self.r1[s, x, z] + self.full[s, x, z, self.core]
                    return 0

                lax.fori_loop(0, self.depth, body, 0)
        self.by_core(lambda core: self.first_copy(core).start())

    def step2(self):
        def act(core):
            self.first_copy(core).wait_recv()

            def body(z, _):
                for h in range(2):
                    mine = self.r1[h, self.gx, z] if core == 0 else self.r1[self.seg, h, z]
                    self.r2[h, z] = self.r2[h, z] + mine
                return 0

            lax.fori_loop(0, self.depth, body, 0)
            self.second_copy(core).start()

        self.by_core(act)

    def step3(self):
        def act(core):
            self.second_copy(core).wait_recv()
            mine = self.seg if core == 0 else self.gx

            def body(z, _):
                self.r3[z] = self.r3[z] + self.r2[mine, z]
                return 0

            lax.fori_loop(0, self.depth, body, 0)

        self.by_core(act)
        for step in range(1, self.depth):
            self.last_copy(step).start()

    def step4(self):
        total = self.r3[self.z].astype(F32)
        for step in range(1, self.depth):
            self.last_copy(step).wait_recv()
            total = total + self.rz[step - 1].astype(F32)
        return total

    def sent(self):
        self.core_copy().wait_send()
        self.by_core(lambda core: self.first_copy(core).wait_send())
        self.by_core(lambda core: self.second_copy(core).wait_send())
        for step in range(1, self.depth):
            self.last_copy(step).wait_send()


def layer_kernel(sizes, pieces, scatter, *refs):
    (node, edge, adj, nb, live, sb, wei, weo, wni, wno, nct, ect) = refs[:12]
    node_out, edge_out, node_grad = refs[12:15]
    grads = refs[15:19]
    (out, ext, rct, ret, pre, spread, mixed, hid, slope, unit, scale, gath, hidn, dpren, dyn, dgath,
     dmix, dsum, halo_sems) = refs[19:38]
    rest = refs[38:]
    blocks, block, latent = node.shape
    degree = adj.shape[0] // blocks
    span = degree * block
    rows = blocks * block

    seg, gx, gy = (lax.axis_index(a) for a in AXES)
    barrier = pltpu.get_barrier_semaphore()
    count = 0
    greet = []
    for axis in FACES:
        here = lax.axis_index(axis)
        for step in (1, -1):
            other = here + step
            there = (other >= 0) & (other < sizes[axis])
            greet.append((there, {axis: other}))
            count = count + there.astype(jnp.int32)
    for there, to in greet:

        @pl.when(there)
        def _(to=to):
            pl.semaphore_signal(barrier, inc=1, device_id=to, device_id_type=MESH)

    if scatter:
        core, z, depth = lax.rem(gy, CORES), lax.div(gy, CORES), sizes["gy"] // CORES
        for step in range(1, depth):
            to = {"gy": lax.rem(z + step, depth) * CORES + core}
            pl.semaphore_signal(barrier, inc=1, device_id=to, device_id_type=MESH)
        count = count + (depth - 1)
    pl.semaphore_wait(barrier, count)

    for j in range(6):
        out[j] = node[sb[0, j]]
    ahead = Halo(out, ext.at[pl.ds(blocks, 6)], halo_sems, 0, sizes)
    ahead.start()
    ahead.zero()

    if scatter:
        per = len(rest) // 2
        del per
        fulls, bufs, sems = rest[0:3], rest[3:15], rest[15]
        moves = [
            Scatter(fulls[i], *bufs[4 * i : 4 * i + 4], sems, i, sizes) for i in range(3)
        ]

    def put(piece, row, value, part=0):
        if not scatter:
            grads[piece][row : row + value.shape[0], :] = value.astype(BF16)
            return
        index, base = pieces[piece]
        own = grads[piece].shape[0]
        value = value.astype(BF16)
        depth = sizes["gy"] // CORES
        for t in range(0, value.shape[0], TILE):
            d, at = divmod(row + t, own)
            d, c = divmod(d, CORES)
            d, z = divmod(d, depth)
            s, x = divmod(d, sizes["gx"])
            fulls[index][s, x, z, c, base + at : base + at + TILE, :] = value[t : t + TILE]

    def weight_grad(piece, row, left, right):
        half = latent // 2
        for h in range(2):
            put(piece, row + h * half, mm_tn(left[:, h * half : (h + 1) * half], right[...]))

    for n in range(blocks):
        ext[n] = node[n]

    def first(n, _):
        at = pl.multiple_of(n * span, span)
        own = mm(node[n], wei[latent : 2 * latent, :])
        whole = mm(edge[pl.ds(at, span), :], wei[:latent, :])
        for k in range(degree):
            pre[pl.ds(pl.multiple_of(at + k * block, block), block), :] = (
                whole[k * block : (k + 1) * block] + own
            )
        return 0

    lax.fori_loop(0, blocks, first, 0)

    def picked(n, _):
        at = pl.multiple_of(n * span, span)
        for k in range(degree):
            turned = adj[n * degree + k].T
            for j in range(blocks + 6):
                pick = jnp.where(nb[n, k] == j, 1.0, 0.0).astype(F32)
                spread[j * block : (j + 1) * block, pl.ds(pl.multiple_of(at + k * block, block), block)] = (
                    turned.astype(F32) * pick
                ).astype(BF16)
        return 0

    lax.fori_loop(0, blocks, picked, 0)

    ahead.arrive()

    def forward(n, _):
        at = pl.multiple_of(n * span, span)
        here = pl.ds(at, span)
        mix = jnp.concatenate(
            [mm(adj[n * degree + k], ext[nb[n, k]]) for k in range(degree)], axis=0
        ).astype(BF16)
        mixed[here, :] = mix
        value, bend = silu_and_slope(pre[here, :] + mm(mix, wei[2 * latent :, :]))
        value = value.astype(BF16)
        hid[here, :] = value
        slope[here, :] = bend
        message, spreadness = normalised(mm(value, weo[...]))
        unit[here, :] = message
        scale[here, :] = jnp.broadcast_to(spreadness, (span, scale.shape[1]))
        edge_out[here, :] = (edge[here, :].astype(F32) + message).astype(BF16)
        total = message[:block] * live[n, 0].astype(F32)
        for k in range(1, degree):
            total = total + message[k * block : (k + 1) * block] * live[n, k].astype(F32)
        gath[pl.ds(pl.multiple_of(n * block, block), block), :] = total.astype(BF16)
        return 0

    lax.fori_loop(0, blocks, forward, 0)

    group = 2 if blocks % 2 == 0 else 1
    tall = group * block

    def nodes(g, _):
        at = pl.multiple_of(g * tall, tall)
        here = pl.ds(at, tall)
        latents = jnp.concatenate([node[g * group + i] for i in range(group)], axis=0)
        value, bend = silu_and_slope(
            mm(latents, wni[:latent, :]) + mm(gath[here, :], wni[latent:, :])
        )
        value = value.astype(BF16)
        hidn[here, :] = value
        update, spreadness = normalised(mm(value, wno[...]))
        node_out[here, :] = (latents.astype(F32) + update).astype(BF16)
        ct = nct[here, :].astype(F32)
        dy = normalised_ct(ct, update, spreadness).astype(BF16)
        dyn[here, :] = dy
        dp = (mm_nt(dy, wno[...]) * bend).astype(BF16)
        dpren[here, :] = dp
        node_grad[here, :] = ct + mm_nt(dp, wni[:latent, :])
        dgath[here, :] = mm_nt(dp, wni[latent:, :])
        return 0

    lax.fori_loop(0, blocks // group, nodes, 0)

    flat = ext.at[pl.ds(0, blocks)][...].reshape(rows, latent)
    weight_grad(2, 0, flat, dpren)
    weight_grad(2, latent, gath, dpren)
    weight_grad(3, 0, hidn, dyn)
    if scatter:
        moves[0].start()

    def backward(n, _):
        at = pl.multiple_of(n * span, span)
        here = pl.ds(at, span)
        back = dgath[pl.ds(pl.multiple_of(n * block, block), block), :]
        ct = ect[here, :].astype(F32) + jnp.concatenate(
            [back * live[n, k].astype(F32) for k in range(degree)], axis=0
        )
        dy = normalised_ct(ct, unit[here, :], scale[here, :1]).astype(BF16)
        unit[here, :] = dy.astype(F32)
        dp = mm_nt(dy, weo[...]) * slope[here, :]
        total = dp[:block]
        for k in range(1, degree):
            total = total + dp[k * block : (k + 1) * block]
        dsum[pl.ds(pl.multiple_of(n * block, block), block), :] = total.astype(BF16)
        dp = dp.astype(BF16)
        pre[here, :] = dp.astype(F32)
        dmix[here, :] = mm_nt(dp, wei[2 * latent :, :]).astype(BF16)
        return 0

    half = blocks // 2
    lax.fori_loop(0, half, backward, 0)
    if scatter:
        moves[0].step1()
    lax.fori_loop(half, blocks, backward, 0)

    for j in range(6):
        at = (blocks + j) * block
        rct[j] = mm(spread[at : at + block, :], dmix[...]).astype(BF16)
    behind = Halo(rct, ret, halo_sems, 6, sizes)
    behind.start()
    behind.zero()

    weight_grad(1, 0, hid, unit[...].astype(BF16))
    if scatter:
        moves[1].start()
    dp = pre[...].astype(BF16)
    weight_grad(0, 0, edge, dp)
    if scatter:
        moves[0].step2()
        moves[1].step1()
    weight_grad(0, latent, flat, dsum)
    weight_grad(0, 2 * latent, mixed, dp)
    if scatter:
        moves[2].start()

    node_grad[...] += mm(spread[: blocks * block, :], dmix[...]) + mm_nt(
        dsum[...], wei[latent : 2 * latent, :]
    )
    if scatter:
        moves[2].step1()
        moves[0].step3()
        moves[1].step2()

    behind.arrive()
    for n in range(blocks):
        total = node_grad[n * block : (n + 1) * block, :]
        for j in range(6):
            pick = jnp.where(sb[0, j] == n, 1.0, 0.0).astype(F32)
            total = total + ret[j].astype(F32) * pick
        node_grad[n * block : (n + 1) * block, :] = total

    if scatter:
        moves[1].step3()
        moves[2].step2()
        nodes_total = moves[0].step4()
        own = grads[2].shape[0]
        grads[2][...] = nodes_total[:own]
        grads[3][...] = nodes_total[own:]
        grads[1][...] = moves[1].step4()
        moves[2].step3()
        grads[0][...] = moves[2].step4()
        for move in moves:
            move.sent()
    ahead.sent()
    behind.sent()


def layer(sizes, *args):
    (node, edge, adj, nb, live, sb, wei, weo, wni, wno, nct, ect) = args
    rows, latent = node.shape
    blocks, degree = nb.shape
    block = adj.shape[-1]
    edges = edge.shape[0]
    devices = sizes["segment"] * sizes["gx"] * sizes["gy"]
    weights = (wei, weo, wni, wno)
    scatter = (
        sizes["segment"] == 2
        and sizes["gx"] == 2
        and sizes["gy"] % CORES == 0
        and all(w.shape[0] % (devices * TILE) == 0 for w in weights)
    )
    shapes = [
        jax.ShapeDtypeStruct((rows, latent), BF16),
        jax.ShapeDtypeStruct((edges, latent), BF16),
        jax.ShapeDtypeStruct((rows, latent), F32),
    ]
    scratch = [
        pltpu.VMEM((6, block, latent), BF16),
        pltpu.VMEM((blocks + 6, block, latent), BF16),
        pltpu.VMEM((6, block, latent), BF16),
        pltpu.VMEM((6, block, latent), BF16),
        pltpu.VMEM((edges, latent), F32),
        pltpu.VMEM(((blocks + 6) * block, edges), BF16),
        pltpu.VMEM((edges, latent), BF16),
        pltpu.VMEM((edges, latent), BF16),
        pltpu.VMEM((edges, latent), F32),
        pltpu.VMEM((edges, latent), F32),
        pltpu.VMEM((edges, 128), F32),
        pltpu.VMEM((rows, latent), BF16),
        pltpu.VMEM((rows, latent), BF16),
        pltpu.VMEM((rows, latent), BF16),
        pltpu.VMEM((rows, latent), BF16),
        pltpu.VMEM((rows, latent), F32),
        pltpu.VMEM((edges, latent), BF16),
        pltpu.VMEM((rows, latent), BF16),
        pltpu.SemaphoreType.DMA((2, 12)),
    ]
    pieces = None
    if scatter:
        own = [w.shape[0] // devices for w in weights]
        shapes += [jax.ShapeDtypeStruct((r, latent), F32) for r in own]
        pieces = {2: (0, 0), 3: (0, own[2]), 1: (1, 0), 0: (2, 0)}
        s, x, z = sizes["segment"], sizes["gx"], sizes["gy"] // CORES
        heights = (own[2] + own[3], own[1], own[0])
        scratch += [pltpu.VMEM((s, x, z, CORES, r, latent), BF16) for r in heights]
        for r in heights:
            scratch += [
                pltpu.VMEM((s, x, z, r, latent), BF16),
                pltpu.VMEM((2, z, r, latent), BF16),
                pltpu.VMEM((z, r, latent), BF16),
                pltpu.VMEM((z - 1, r, latent), BF16),
            ]
        scratch.append(pltpu.SemaphoreType.DMA((2, 3, 2 + z)))
    else:
        shapes += [jax.ShapeDtypeStruct(w.shape, BF16) for w in weights]
    vmem = pl.BlockSpec(memory_space=pltpu.VMEM)
    smem = pl.BlockSpec(memory_space=pltpu.SMEM)
    results = pl.pallas_call(
        functools.partial(layer_kernel, sizes, pieces, scatter),
        out_shape=shapes,
        in_specs=[vmem, vmem, vmem, smem, smem, smem] + [vmem] * 6,
        out_specs=[vmem] * 7,
        scratch_shapes=scratch,
        compiler_params=pltpu.CompilerParams(
            collective_id=0, has_side_effects=True, vmem_limit_bytes=60 * 1024 * 1024
        ),
    )(
        node.reshape(blocks, block, latent),
        edge,
        adj.reshape(blocks * degree, block, block),
        nb,
        live,
        sb,
        wei,
        weo,
        wni,
        wno,
        nct,
        ect,
    )
    shares = results[3:]
    if scatter:
        shares = [g.reshape(-1) for g in shares]
    else:
        shares = [
            lax.psum_scatter(g.astype(F32).reshape(-1), AXES, scatter_dimension=0, tiled=True)
            for g in shares
        ]
    return tuple(results[:3]) + tuple(shares)


def solution(mesh):
    split, copied = P(AXES, None), P()
    return jax.shard_map(
        functools.partial(layer, dict(mesh.shape)),
        mesh=mesh,
        in_specs=(split, split, P(AXES, None, None, None), split, split, split)
        + (copied,) * 4
        + (split, split),
        out_specs=(split, split, split) + (P(AXES),) * 4,
        check_vma=False,
    )
```

time: 285 us -> 67 us (0.24)
  waiting for transfers between devices: 127 us -> 0 us
  Pallas kernels: 0 us -> 53.6 us
  local copies, waits for them, and re-layouts: 60.7 us -> 12.5 us
  matrix products: 36.8 us -> 0 us
  starting transfers between devices: 33.4 us -> 0 us
  between operations: 14.7 us -> 0.65 us
  other arithmetic: 10.1 us -> 0 us
    unnamed x2 -> x0, waiting for transfers between devices: 127 us -> none
    pallas_call x0 -> x1, Pallas kernels: none -> 53.6 us  [layer(): pl.pallas_call(functools.partial(layer_kernel, sizes, pieces, scatter), o...]
    dot_general x26 -> x0, matrix products: 36.8 us -> none  [the longest x3 5.26 us: edge_part(): jnp.dot(node_blocks.reshape(-1, latent), w_edge_in[latent:2 * latent], pr...]
    ppermute x12 -> x0, starting transfers between devices: 33.3 us -> none  [passed_along(): return lax.ppermute(block, axis, route)]
    another operation x13 -> x0, local copies, waits for them, and re-layouts: 20.2 us -> none  [swap_faces(): jnp.stack([across_rows(face_blocks[1], 1), across_rows(face_blocks[0], -1...]
    concatenate x1 -> x0, local copies, waits for them, and re-layouts: 10.9 us -> none  [edge_part(): extended = jnp.concatenate([node_blocks, received], axis=0)]
    unnamed x84 -> x13, local copies, waits for them, and re-layouts: 22.8 us -> 12.5 us
    reduce_sum x7 -> x0, other arithmetic: 5.71 us -> none  [the longest x2 2.71 us: layer_norm(): centred = values - average]
  transfers between devices with their start and end apart: 13 -> 0, of which waited for: 1 -> 0; matrix products, arithmetic and copies ran while one was open for 17% -> 0% of each run, Pallas kernels for 0% -> 0%
where the time goes in v1:
time: 67 us; the launch traced here: 66.7 us
  Pallas kernels  53.6 us (80%)
  local copies, waits for them, and re-layouts  12.5 us (19%)
    pallas_call x1, Pallas kernels, layer(): pl.pallas_call(functools.partial(layer_kernel, sizes, pieces, scatter), o...  53.6 us
    unnamed x13, local copies, waits for them, and re-layouts  12.5 us

profile of v1, /device:TPU:0, one launch (start us, length us, event | category | flops | bytes accessed | tf_op | source)
XLA Modules:
  0.0 66.7 jit_solution(11124605383877514597)
XLA Ops:
  0.6 1.3 %copy.19.refs_3_ = s32[4,2]{1,0:T(4,128)} copy(s32[4,2]{0,1:T(2,128)} %param.15) | data formatting | bytes 64 | tf_op args[3]
  2.0 1.3 %copy.20.refs_4_ = s32[4,2]{1,0:T(4,128)} copy(s32[4,2]{0,1:T(2,128)} %param.16) | data formatting | bytes 64 | tf_op args[4]
  3.3 53.6 %shard_map.171 = (bf16[512,512]{1,0:T(8,128)(2,1)}, bf16[1024,512]{1,0:T(8,128)(2,1)}, f32[512,512]{1,0:T(8,128)}, f32[48,512]{1,0:T(8,128)}, f32[16,512]{1,0:T(...) custom-call(bf16[4,128,512]{2,1,0:T(8,128)(2,1)} %bitcast.10, bf16[1024,512]{1,0:T(8,128)(2,1)} %refs_1_.1, ...), custom_call_target="tpu_custom_call" | custom-call | tf_op jit(solution)/shard_map/pallas_call | solution.py:490
  56.9 0.0 copy-start.1
  56.9 1.5 %copy.22 = f32[2,4,8,128]{3,1,2,0:T(4,128)} copy(f32[2,4,8,128]{3,2,1,0:T(8,128)} %bitcast.19) | data formatting | bytes 65536
  58.4 1.4 %copy.24 = f32[2,4,8,128]{3,1,2,0:T(4,128)} copy(f32[2,4,8,128]{3,2,1,0:T(8,128)} %bitcast.18) | data formatting | bytes 65536
  59.8 1.5 %copy.23 = f32[4,4,8,128]{3,1,2,0:T(4,128)} copy(f32[4,4,8,128]{3,2,1,0:T(8,128)} %bitcast.15) | data formatting | bytes 131072
  61.3 1.6 %copy.21 = f32[6,4,8,128]{3,1,2,0:T(4,128)} copy(f32[6,4,8,128]{3,2,1,0:T(8,128)} %bitcast.13) | data formatting | bytes 196608
  62.8 0.0 copy-start
  62.8 2.0 %copy.28 = bf16[512,512]{1,0:T(8,128)(2,1)} copy(bf16[512,512]{1,0:T(8,128)(2,1)} %get-tuple-element.28) | data formatting | bytes 1048576
  64.8 0.0 copy-done.1
  64.8 1.0 %copy.29 = bf16[1024,512]{1,0:T(8,128)(2,1)} copy(bf16[1024,512]{1,0:T(8,128)(2,1)S(1)} %copy-done.1) | data formatting | bytes 2097152
  65.7 0.0 copy-done
  65.7 1.0 %copy.30 = f32[512,512]{1,0:T(8,128)} copy(f32[512,512]{1,0:T(8,128)S(1)} %copy-done) | data formatting | bytes 2097152
Async XLA Ops:
  56.9 7.9 %copy-start.1 = (bf16[1024,512]{1,0:T(8,128)(2,1)S(1)}, bf16[1024,512]{1,0:T(8,128)(2,1)}, u32[]{:S(2)}) copy-start(bf16[1024,512]{1,0:T(8,128)(2,1)} %get-tuple-element.29) | copy-start | bytes 3145732
  62.8 2.9 %copy-start = (f32[512,512]{1,0:T(8,128)S(1)}, f32[512,512]{1,0:T(8,128)}, u32[]{:S(2)}) copy-start(f32[512,512]{1,0:T(8,128)} %get-tuple-element.30) | copy-start | bytes 3145732

commit v2 on v1

--- a/solution.py
+++ b/solution.py
@@ -141,25 +141,18 @@
         self.core_copy().wait_recv()
         for s in range(2):
             for x in range(2):
-
-                def body(z, _):
+                for z in range(self.depth):
                     self.r1[s, x, z] = self.r1[s, x, z] + self.full[s, x, z, self.core]
-                    return 0
-
-                lax.fori_loop(0, self.depth, body, 0)
         self.by_core(lambda core: self.first_copy(core).start())
 
     def step2(self):
         def act(core):
             self.first_copy(core).wait_recv()
 
-            def body(z, _):
+            for z in range(self.depth):
                 for h in range(2):
                     mine = self.r1[h, self.gx, z] if core == 0 else self.r1[self.seg, h, z]
                     self.r2[h, z] = self.r2[h, z] + mine
-                return 0
-
-            lax.fori_loop(0, self.depth, body, 0)
             self.second_copy(core).start()
 
         self.by_core(act)
@@ -169,11 +162,8 @@
             self.second_copy(core).wait_recv()
             mine = self.seg if core == 0 else self.gx
 
-            def body(z, _):
+            for z in range(self.depth):
                 self.r3[z] = self.r3[z] + self.r2[mine, z]
-                return 0
-
-            lax.fori_loop(0, self.depth, body, 0)
 
         self.by_core(act)
         for step in range(1, self.depth):
@@ -194,19 +184,27 @@
             self.last_copy(step).wait_send()
 
 
-def layer_kernel(sizes, pieces, scatter, *refs):
-    (node, edge, adj, nb, live, sb, wei, weo, wni, wno, nct, ect) = refs[:12]
-    node_out, edge_out, node_grad = refs[12:15]
+def layer_kernel(sizes, plan, scatter, *refs):
+    nb, live, sb = refs[:3]
+    operands = refs[3:12]
+    node_out_hbm, edge_out_hbm, node_grad = refs[12:15]
     grads = refs[15:19]
-    (out, ext, rct, ret, pre, spread, mixed, hid, slope, unit, scale, gath, hidn, dpren, dyn, dgath,
-     dmix, dsum, halo_sems) = refs[19:38]
-    rest = refs[38:]
+    held = refs[19:28]
+    (node, edge, wei, adj, weo, wni, wno, nct, ect) = held
+    (node_out, edge_out, out, ext, rct, ret, pre, spread, mixed, hid, slope, unit, scale, gath, hidn,
+     dpren, dyn, dgath, dmix, dsum, dye, dpe, load_sems, halo_sems) = refs[28:52]
+    rest = refs[52:]
     blocks, block, latent = node.shape
     degree = adj.shape[0] // blocks
     span = degree * block
     rows = blocks * block
 
-    seg, gx, gy = (lax.axis_index(a) for a in AXES)
+    loads = {}
+    for i, (src, dst) in enumerate(zip(operands, held)):
+        loads[i] = pltpu.make_async_copy(src, dst, load_sems.at[i])
+        loads[i].start()
+
+    gy = lax.axis_index("gy")
     barrier = pltpu.get_barrier_semaphore()
     count = 0
     greet = []
@@ -229,97 +227,116 @@
             to = {"gy": lax.rem(z + step, depth) * CORES + core}
             pl.semaphore_signal(barrier, inc=1, device_id=to, device_id_type=MESH)
         count = count + (depth - 1)
-    pl.semaphore_wait(barrier, count)
-
+    loads[0].wait()
     for j in range(6):
         out[j] = node[sb[0, j]]
+    pl.semaphore_wait(barrier, count)
+
     ahead = Halo(out, ext.at[pl.ds(blocks, 6)], halo_sems, 0, sizes)
     ahead.start()
     ahead.zero()
 
-    if scatter:
-        per = len(rest) // 2
-        del per
-        fulls, bufs, sems = rest[0:3], rest[3:15], rest[15]
+    moves = []
+    if scatter:
+        pieces, starts, total = plan
+        fulls, bufs, sems = rest[:total], rest[total : 5 * total], rest[5 * total]
         moves = [
-            Scatter(fulls[i], *bufs[4 * i : 4 * i + 4], sems, i, sizes) for i in range(3)
+            Scatter(fulls[i], *bufs[4 * i : 4 * i + 4], sems, i, sizes) for i in range(total)
         ]
 
-    def put(piece, row, value, part=0):
+    def put(weight, row, value):
+        value = value.astype(BF16)
         if not scatter:
-            grads[piece][row : row + value.shape[0], :] = value.astype(BF16)
+            grads[weight][row : row + value.shape[0], :] = value
             return
-        index, base = pieces[piece]
-        own = grads[piece].shape[0]
-        value = value.astype(BF16)
+        own = starts[weight]
         depth = sizes["gy"] // CORES
         for t in range(0, value.shape[0], TILE):
             d, at = divmod(row + t, own)
             d, c = divmod(d, CORES)
             d, z = divmod(d, depth)
             s, x = divmod(d, sizes["gx"])
-            fulls[index][s, x, z, c, base + at : base + at + TILE, :] = value[t : t + TILE]
-
-    def weight_grad(piece, row, left, right):
-        half = latent // 2
-        for h in range(2):
-            put(piece, row + h * half, mm_tn(left[:, h * half : (h + 1) * half], right[...]))
-
+            index, base = pieces[weight, at // TILE]
+            fulls[index][s, x, z, c, base : base + TILE, :] = value[t : t + TILE]
+
+    def give_piece(index, value):
+        for (weight, sub), (piece, base) in pieces.items():
+            if piece == index:
+                ratio = latent // 128
+                for q in range(ratio):
+                    part = value[base : base + TILE, q * 128 : (q + 1) * 128]
+                    at = sub * TILE * ratio + q
+                    grads[weight][pl.ds(at, TILE, stride=ratio), :] = part
+
+    group = 2 if blocks % 2 == 0 else 1
+    tall = group * block
+    wide = group * span
+
+    loads[1].wait()
+    loads[2].wait()
     for n in range(blocks):
         ext[n] = node[n]
 
-    def first(n, _):
-        at = pl.multiple_of(n * span, span)
-        own = mm(node[n], wei[latent : 2 * latent, :])
-        whole = mm(edge[pl.ds(at, span), :], wei[:latent, :])
+    def first(g, _):
+        at = pl.multiple_of(g * wide, wide)
+        latents = jnp.concatenate([node[g * group + i] for i in range(group)], axis=0)
+        own = mm(latents, wei[latent : 2 * latent, :])
+        whole = mm(edge[pl.ds(at, wide), :], wei[:latent, :])
+        for i in range(group):
+            for k in range(degree):
+                off = i * span + k * block
+                pre[pl.ds(pl.multiple_of(at + off, block), block), :] = (
+                    whole[off : off + block] + own[i * block : (i + 1) * block]
+                )
+        return 0
+
+    lax.fori_loop(0, blocks // group, first, 0)
+    loads[3].wait()
+
+    def picked(n, _):
         for k in range(degree):
-            pre[pl.ds(pl.multiple_of(at + k * block, block), block), :] = (
-                whole[k * block : (k + 1) * block] + own
-            )
+            turned = adj[n * degree + k].T.astype(F32)
+            col = pl.ds(pl.multiple_of(n * span + k * block, block), block)
+            for j in range(blocks + 6):
+                pick = jnp.where(nb[k, n] == j, 1.0, 0.0).astype(F32)
+                spread[j * block : (j + 1) * block, col] = (turned * pick).astype(BF16)
         return 0
 
-    lax.fori_loop(0, blocks, first, 0)
-
-    def picked(n, _):
-        at = pl.multiple_of(n * span, span)
-        for k in range(degree):
-            turned = adj[n * degree + k].T
-            for j in range(blocks + 6):
-                pick = jnp.where(nb[n, k] == j, 1.0, 0.0).astype(F32)
-                spread[j * block : (j + 1) * block, pl.ds(pl.multiple_of(at + k * block, block), block)] = (
-                    turned.astype(F32) * pick
-                ).astype(BF16)
-        return 0
-
     lax.fori_loop(0, blocks, picked, 0)
-
+    loads[4].wait()
     ahead.arrive()
 
-    def forward(n, _):
-        at = pl.multiple_of(n * span, span)
-        here = pl.ds(at, span)
-        mix = jnp.concatenate(
-            [mm(adj[n * degree + k], ext[nb[n, k]]) for k in range(degree)], axis=0
-        ).astype(BF16)
-        mixed[here, :] = mix
-        value, bend = silu_and_slope(pre[here, :] + mm(mix, wei[2 * latent :, :]))
+    def forward(g, _):
+        at = pl.multiple_of(g * wide, wide)
+        here = pl.ds(at, wide)
+        for i in range(group):
+            n = g * group + i
+            for k in range(degree):
+                off = pl.multiple_of(at + i * span + k * block, block)
+                mixed[pl.ds(off, block), :] = mm(adj[n * degree + k], ext[nb[k, n]]).astype(BF16)
+        value, bend = silu_and_slope(pre[here, :] + mm(mixed[here, :], wei[2 * latent :, :]))
         value = value.astype(BF16)
         hid[here, :] = value
         slope[here, :] = bend
         message, spreadness = normalised(mm(value, weo[...]))
         unit[here, :] = message
-        scale[here, :] = jnp.broadcast_to(spreadness, (span, scale.shape[1]))
+        scale[here, :] = jnp.broadcast_to(spreadness, (wide, scale.shape[1]))
         edge_out[here, :] = (edge[here, :].astype(F32) + message).astype(BF16)
-        total = message[:block] * live[n, 0].astype(F32)
-        for k in range(1, degree):
-            total = total + message[k * block : (k + 1) * block] * live[n, k].astype(F32)
-        gath[pl.ds(pl.multiple_of(n * block, block), block), :] = total.astype(BF16)
+        for i in range(group):
+            n = g * group + i
+            off = i * span
+            total = message[off : off + block] * live[0, n].astype(F32)
+            for k in range(1, degree):
+                part = message[off + k * block : off + (k + 1) * block]
+                total = total + part * live[k, n].astype(F32)
+            gath[pl.ds(pl.multiple_of(n * block, block), block), :] = total.astype(BF16)
         return 0
 
-    lax.fori_loop(0, blocks, forward, 0)
-
-    group = 2 if blocks % 2 == 0 else 1
-    tall = group * block
+    lax.fori_loop(0, blocks // group, forward, 0)
+    edge_done = pltpu.make_async_copy(edge_out, edge_out_hbm, load_sems.at[9])
+    edge_done.start()
+    for i in (5, 6, 7):
+        loads[i].wait()
 
     def nodes(g, _):
         at = pl.multiple_of(g * tall, tall)
@@ -342,66 +359,82 @@
         return 0
 
     lax.fori_loop(0, blocks // group, nodes, 0)
+    node_done = pltpu.make_async_copy(node_out, node_out_hbm, load_sems.at[10])
+    node_done.start()
 
     flat = ext.at[pl.ds(0, blocks)][...].reshape(rows, latent)
-    weight_grad(2, 0, flat, dpren)
-    weight_grad(2, latent, gath, dpren)
-    weight_grad(3, 0, hidn, dyn)
+    put(2, 0, mm_tn(flat, dpren[...]))
+    put(2, latent, mm_tn(gath[...], dpren[...]))
+    put(3, 0, mm_tn(hidn[...], dyn[...]))
     if scatter:
         moves[0].start()
-
-    def backward(n, _):
-        at = pl.multiple_of(n * span, span)
-        here = pl.ds(at, span)
-        back = dgath[pl.ds(pl.multiple_of(n * block, block), block), :]
+    loads[8].wait()
+
+    def backward(g, _):
+        at = pl.multiple_of(g * wide, wide)
+        here = pl.ds(at, wide)
+        back = dgath[pl.ds(pl.multiple_of(g * tall, tall), tall), :]
         ct = ect[here, :].astype(F32) + jnp.concatenate(
-            [back * live[n, k].astype(F32) for k in range(degree)], axis=0
+            [
+                back[i * block : (i + 1) * block] * live[k, g * group + i].astype(F32)
+                for i in range(group)
+                for k in range(degree)
+            ],
+            axis=0,
         )
         dy = normalised_ct(ct, unit[here, :], scale[here, :1]).astype(BF16)
-        unit[here, :] = dy.astype(F32)
+        dye[here, :] = dy
         dp = mm_nt(dy, weo[...]) * slope[here, :]
-        total = dp[:block]
-        for k in range(1, degree):
-            total = total + dp[k * block : (k + 1) * block]
-        dsum[pl.ds(pl.multiple_of(n * block, block), block), :] = total.astype(BF16)
+        for i in range(group):
+            off = i * span
+            total = dp[off : off + block]
+            for k in range(1, degree):
+                total = total + dp[off + k * block : off + (k + 1) * block]
+            dsum[pl.ds(pl.multiple_of((g * group + i) * block, block), block), :] = total.astype(BF16)
         dp = dp.astype(BF16)
-        pre[here, :] = dp.astype(F32)
+        dpe[here, :] = dp
         dmix[here, :] = mm_nt(dp, wei[2 * latent :, :]).astype(BF16)
         return 0
 
-    half = blocks // 2
+    half = (blocks // group) // 2
     lax.fori_loop(0, half, backward, 0)
     if scatter:
         moves[0].step1()
-    lax.fori_loop(half, blocks, backward, 0)
-
+    lax.fori_loop(half, blocks // group, backward, 0)
+
+    put(1, 0, mm_tn(hid[...], dye[...]))
+    late = moves[2:]
+    if scatter:
+        moves[1].start()
+        moves[0].step2()
+    put(0, 0, mm_tn(edge[...], dpe[...]))
+    put(0, latent, mm_tn(flat, dsum[...]))
+    put(0, 2 * latent, mm_tn(mixed[...], dpe[...]))
+    for move in late:
+        move.start()
+    if scatter:
+        moves[1].step1()
+
+    returns = mm(spread[rows:, :], dmix[...]).astype(BF16)
     for j in range(6):
-        at = (blocks + j) * block
-        rct[j] = mm(spread[at : at + block, :], dmix[...]).astype(BF16)
+        rct[j] = returns[j * block : (j + 1) * block]
     behind = Halo(rct, ret, halo_sems, 6, sizes)
     behind.start()
     behind.zero()
 
-    weight_grad(1, 0, hid, unit[...].astype(BF16))
-    if scatter:
-        moves[1].start()
-    dp = pre[...].astype(BF16)
-    weight_grad(0, 0, edge, dp)
-    if scatter:
-        moves[0].step2()
-        moves[1].step1()
-    weight_grad(0, latent, flat, dsum)
-    weight_grad(0, 2 * latent, mixed, dp)
-    if scatter:
-        moves[2].start()
-
-    node_grad[...] += mm(spread[: blocks * block, :], dmix[...]) + mm_nt(
+    for move in late:
+        move.step1()
+    if scatter:
+        moves[0].step3()
+    node_grad[...] += mm(spread[:rows, :], dmix[...]) + mm_nt(
         dsum[...], wei[latent : 2 * latent, :]
     )
     if scatter:
-        moves[2].step1()
-        moves[0].step3()
         moves[1].step2()
+        for move in late:
+            move.step2()
+        give_piece(0, moves[0].step4())
+        moves[1].step3()
 
     behind.arrive()
     for n in range(blocks):
@@ -411,20 +444,29 @@
             total = total + ret[j].astype(F32) * pick
         node_grad[n * block : (n + 1) * block, :] = total
 
-    if scatter:
-        moves[1].step3()
-        moves[2].step2()
-        nodes_total = moves[0].step4()
-        own = grads[2].shape[0]
-        grads[2][...] = nodes_total[:own]
-        grads[3][...] = nodes_total[own:]
-        grads[1][...] = moves[1].step4()
-        moves[2].step3()
-        grads[0][...] = moves[2].step4()
-        for move in moves:
-            move.sent()
+    for move in late:
+        move.step3()
+    if scatter:
+        give_piece(1, moves[1].step4())
+    for i, move in enumerate(late):
+        give_piece(2 + i, move.step4())
+    for move in moves:
+        move.sent()
     ahead.sent()
     behind.sent()
+    edge_done.wait()
+    node_done.wait()
+
+
+def hand_over(*refs):
+    count = (len(refs) - 1) // 2
+    copies = [
+        pltpu.make_async_copy(refs[i], refs[count + i], refs[-1].at[i]) for i in range(count)
+    ]
+    for copy in copies:
+        copy.start()
+    for copy in copies:
+        copy.wait()
 
 
 def layer(sizes, *args):
@@ -446,7 +488,21 @@
         jax.ShapeDtypeStruct((edges, latent), BF16),
         jax.ShapeDtypeStruct((rows, latent), F32),
     ]
-    scratch = [
+    operands = (
+        node.reshape(blocks, block, latent),
+        edge,
+        wei,
+        adj.reshape(blocks * degree, block, block),
+        weo,
+        wni,
+        wno,
+        nct,
+        ect,
+    )
+    scratch = [pltpu.VMEM(a.shape, a.dtype) for a in operands]
+    scratch += [
+        pltpu.VMEM((rows, latent), BF16),
+        pltpu.VMEM((edges, latent), BF16),
         pltpu.VMEM((6, block, latent), BF16),
         pltpu.VMEM((blocks + 6, block, latent), BF16),
         pltpu.VMEM((6, block, latent), BF16),
@@ -465,15 +521,27 @@
         pltpu.VMEM((rows, latent), F32),
         pltpu.VMEM((edges, latent), BF16),
         pltpu.VMEM((rows, latent), BF16),
+        pltpu.VMEM((edges, latent), BF16),
+        pltpu.VMEM((edges, latent), BF16),
+        pltpu.SemaphoreType.DMA((11,)),
         pltpu.SemaphoreType.DMA((2, 12)),
     ]
-    pieces = None
+    plan = None
     if scatter:
         own = [w.shape[0] // devices for w in weights]
-        shapes += [jax.ShapeDtypeStruct((r, latent), F32) for r in own]
-        pieces = {2: (0, 0), 3: (0, own[2]), 1: (1, 0), 0: (2, 0)}
+        shapes += [jax.ShapeDtypeStruct((r * latent // 128, 128), F32) for r in own]
+        pieces = {}
+        for sub in range(own[2] // TILE):
+            pieces[2, sub] = (0, sub * TILE)
+        for sub in range(own[3] // TILE):
+            pieces[3, sub] = (0, own[2] + sub * TILE)
+        for sub in range(own[1] // TILE):
+            pieces[1, sub] = (1, sub * TILE)
+        for sub in range(own[0] // TILE):
+            pieces[0, sub] = (2 + sub, 0)
+        heights = [own[2] + own[3], own[1]] + [TILE] * (own[0] // TILE)
+        plan = (pieces, own, len(heights))
         s, x, z = sizes["segment"], sizes["gx"], sizes["gy"] // CORES
-        heights = (own[2] + own[3], own[1], own[0])
         scratch += [pltpu.VMEM((s, x, z, CORES, r, latent), BF16) for r in heights]
         for r in heights:
             scratch += [
@@ -482,41 +550,36 @@
                 pltpu.VMEM((z, r, latent), BF16),
                 pltpu.VMEM((z - 1, r, latent), BF16),
             ]
-        scratch.append(pltpu.SemaphoreType.DMA((2, 3, 2 + z)))
+        scratch.append(pltpu.SemaphoreType.DMA((2, len(heights), 2 + z)))
     else:
         shapes += [jax.ShapeDtypeStruct(w.shape, BF16) for w in weights]
     vmem = pl.BlockSpec(memory_space=pltpu.VMEM)
     smem = pl.BlockSpec(memory_space=pltpu.SMEM)
+    hbm = pl.BlockSpec(memory_space=pl.ANY)
     results = pl.pallas_call(
-        functools.partial(layer_kernel, sizes, pieces, scatter),
+        functools.partial(layer_kernel, sizes, plan, scatter),
         out_shape=shapes,
-        in_specs=[vmem, vmem, vmem, smem, smem, smem] + [vmem] * 6,
-        out_specs=[vmem] * 7,
+        in_specs=[smem] * 3 + [hbm] * len(operands),
+        out_specs=[hbm, hbm] + [vmem] * 5,
         scratch_shapes=scratch,
         compiler_params=pltpu.CompilerParams(
             collective_id=0, has_side_effects=True, vmem_limit_bytes=60 * 1024 * 1024
         ),
-    )(
-        node.reshape(blocks, block, latent),
-        edge,
-        adj.reshape(blocks * degree, block, block),
-        nb,
-        live,
-        sb,
-        wei,
-        weo,
-        wni,
-        wno,
-        nct,
-        ect,
-    )
-    shares = results[3:]
-    if scatter:
-        shares = [g.reshape(-1) for g in shares]
+    )(nb.T, live.T, sb, *operands)
+    if scatter:
+        results = pl.pallas_call(
+            hand_over,
+            out_shape=shapes,
+            in_specs=[hbm] * 7,
+            out_specs=[hbm] * 7,
+            scratch_shapes=[pltpu.SemaphoreType.DMA((7,))],
+            compiler_params=pltpu.CompilerParams(vmem_limit_bytes=60 * 1024 * 1024),
+        )(*results)
+        shares = [g.reshape(-1) for g in results[3:]]
     else:
         shares = [
             lax.psum_scatter(g.astype(F32).reshape(-1), AXES, scatter_dimension=0, tiled=True)
-            for g in shares
+            for g in results[3:]
         ]
     return tuple(results[:3]) + tuple(shares)
 

time: 67 us -> 138 us (2.06)
  Pallas kernels: 53.6 us -> 137 us
  local copies, waits for them, and re-layouts: 12.5 us -> 0 us
    pallas_call x1 -> x2, Pallas kernels: 53.6 us -> 137 us  [the longest x1 87.5 us: layer(): pl.pallas_call(hand_over, out_shape=shapes, in_specs=[hbm] * 7, out_specs...]
    unnamed x13 -> x0, local copies, waits for them, and re-layouts: 12.5 us -> none
where the time goes in v2:
time: 138 us; the launch traced here: 137 us
  Pallas kernels  137 us (99%)
    pallas_call x1, Pallas kernels, layer(): pl.pallas_call(hand_over, out_shape=shapes, in_specs=[hbm] * 7, out_specs...  87.5 us
    pallas_call x1, Pallas kernels, layer(): pl.pallas_call(functools.partial(layer_kernel, sizes, plan, scatter), out...  49.2 us

profile of v2, /device:TPU:0, one launch (start us, length us, event | category | flops | bytes accessed | tf_op | source)
XLA Modules:
  0.0 137.4 jit_solution(4896225972511602305)
XLA Ops:
  0.6 49.2 %shard_map.171 = (bf16[512,512]{1,0:T(8,128)(2,1)}, bf16[1024,512]{1,0:T(8,128)(2,1)}, f32[512,512]{1,0:T(8,128)}, f32[192,128]{1,0:T(8,128)}, f32[64,128]{1,0:T...) custom-call(s32[2,4]{1,0:T(2,128)} %bitcast.10, s32[2,4]{1,0:T(2,128)} %bitcast.11, s32[1,6]{1,0:T(1,128)} %refs_2_.1, ...), custom_call_target="tpu_custom_call" | custom-call | tf_op jit(solution)/shard_map/pallas_call | solution.py:559
  49.8 87.5 %shard_map.172 = (bf16[512,512]{1,0:T(8,128)(2,1)}, bf16[1024,512]{1,0:T(8,128)(2,1)}, f32[512,512]{1,0:T(8,128)}, f32[192,128]{1,0:T(8,128)}, f32[64,128]{1,0:T...) custom-call(bf16[512,512]{1,0:T(8,128)(2,1)} %get-tuple-element.21.refs_0_, bf16[1024,512]{1,0:T(8,128)(2,1)} %get-tuple-element.22.refs_1_, ...), custom_call_target="tpu_custom_call" | custom-call | tf_op jit(solution)/shard_map/pallas_call | solution.py:570

commit v3 on v2

--- a/solution.py
+++ b/solution.py
@@ -402,6 +402,13 @@
         moves[0].step1()
     lax.fori_loop(half, blocks // group, backward, 0)
 
+    returns = mm(spread[rows:, :], dmix[...]).astype(BF16)
+    for j in range(6):
+        rct[j] = returns[j * block : (j + 1) * block]
+    behind = Halo(rct, ret, halo_sems, 6, sizes)
+    behind.start()
+    behind.zero()
+
     put(1, 0, mm_tn(hid[...], dye[...]))
     late = moves[2:]
     if scatter:
@@ -414,13 +421,6 @@
         move.start()
     if scatter:
         moves[1].step1()
-
-    returns = mm(spread[rows:, :], dmix[...]).astype(BF16)
-    for j in range(6):
-        rct[j] = returns[j * block : (j + 1) * block]
-    behind = Halo(rct, ret, halo_sems, 6, sizes)
-    behind.start()
-    behind.zero()
 
     for move in late:
         move.step1()
@@ -459,13 +459,16 @@
 
 
 def hand_over(*refs):
-    count = (len(refs) - 1) // 2
-    copies = [
-        pltpu.make_async_copy(refs[i], refs[count + i], refs[-1].at[i]) for i in range(count)
-    ]
-    for copy in copies:
+    count = (len(refs) - 1) // 3
+    first, last, held, sems = refs[:count], refs[count : 2 * count], refs[2 * count : -1], refs[-1]
+    into = [pltpu.make_async_copy(first[i], held[i], sems.at[0, i]) for i in range(count)]
+    onto = [pltpu.make_async_copy(held[i], last[i], sems.at[1, i]) for i in range(count)]
+    for copy in into:
         copy.start()
-    for copy in copies:
+    for a, b in zip(into, onto):
+        a.wait()
+        b.start()
+    for copy in onto:
         copy.wait()
 
 
@@ -572,7 +575,8 @@
             out_shape=shapes,
             in_specs=[hbm] * 7,
             out_specs=[hbm] * 7,
-            scratch_shapes=[pltpu.SemaphoreType.DMA((7,))],
+            scratch_shapes=[pltpu.VMEM(a.shape, a.dtype) for a in shapes]
+            + [pltpu.SemaphoreType.DMA((2, 7))],
             compiler_params=pltpu.CompilerParams(vmem_limit_bytes=60 * 1024 * 1024),
         )(*results)
         shares = [g.reshape(-1) for g in results[3:]]

time: 138 us -> 52.1 us (0.38)
  Pallas kernels: 137 us -> 51.3 us
    pallas_call x1, Pallas kernels: 87.5 us -> 2.88 us  [layer(): pl.pallas_call(hand_over, out_shape=shapes, in_specs=[hbm] * 7, out_specs...]
where the time goes in v3:
time: 52.1 us; the launch traced here: 51.9 us
  Pallas kernels  51.3 us (98%)
  between operations  0.65 us (1%)
    pallas_call x1, Pallas kernels, layer(): pl.pallas_call(functools.partial(layer_kernel, sizes, plan, scatter), out...  48.4 us
    pallas_call x1, Pallas kernels, layer(): pl.pallas_call(hand_over, out_shape=shapes, in_specs=[hbm] * 7, out_specs...  2.88 us

profile of v3, /device:TPU:0, one launch (start us, length us, event | category | flops | bytes accessed | tf_op | source)
XLA Modules:
  0.0 51.9 jit_solution(3957255379737823250)
XLA Ops:
  0.6 48.4 %shard_map.171 = (bf16[512,512]{1,0:T(8,128)(2,1)}, bf16[1024,512]{1,0:T(8,128)(2,1)}, f32[512,512]{1,0:T(8,128)}, f32[192,128]{1,0:T(8,128)}, f32[64,128]{1,0:T...) custom-call(s32[2,4]{1,0:T(2,128)} %bitcast.10, s32[2,4]{1,0:T(2,128)} %bitcast.11, s32[1,6]{1,0:T(1,128)} %refs_2_.1, ...), custom_call_target="tpu_custom_call" | custom-call | tf_op jit(solution)/shard_map/pallas_call | solution.py:562
  49.1 2.9 %shard_map.172 = (bf16[512,512]{1,0:T(8,128)(2,1)}, bf16[1024,512]{1,0:T(8,128)(2,1)}, f32[512,512]{1,0:T(8,128)}, f32[192,128]{1,0:T(8,128)}, f32[64,128]{1,0:T...) custom-call(bf16[512,512]{1,0:T(8,128)(2,1)} %get-tuple-element.21.refs_0_, bf16[1024,512]{1,0:T(8,128)(2,1)} %get-tuple-element.22.refs_1_, ...), custom_call_target="tpu_custom_call" | custom-call | tf_op jit(solution)/shard_map/pallas_call | solution.py:573
